TPU v7x, 256 devices: a whole 4x4x8 slice. The times are simulated.
256 devices in a mesh: tm: 16 (over z_lo, y, core), rows: 16 (over x, z_hi).
Axes of the slice: x: 4, y: 4, z: 8 (z_hi: 4, z_lo: 2; z = z_hi * 2 + z_lo), core: 2. Of those that a mesh axis runs over, the one named last changes fastest.
Arguments:
- queries: bfloat16 [32, 64, 32, 1536], P('tm', 'rows'), may hold values from -8 to 8
- keys: bfloat16 [32, 64, 32, 1536], P('tm', 'rows'), may hold values from -8 to 8
- values: bfloat16 [32, 64, 32, 1536], P('tm', 'rows'), may hold values from -6 to 6
- win_off: int32 [8, 8, 4, 3], replicated, may hold values from -1 to 1
- row_valid: int32 [8], replicated, may hold values from 1 to 8
Outputs:
- attended: bfloat16 [32, 64, 32, 1536], P('tm', 'rows')
All inputs are finite; a program needn't handle non-finite values.
Results may differ from a plain program's by a relative error of at most 0.0047.
Values may be sent and summed in bfloat16 or wider, within the bound.
A program may use at most 128 MiB of HBM per device.

v0:
```python
import jax
import jax.numpy as jnp
from jax import lax
from jax.sharding import PartitionSpec as P

HEAD_DIM = 128


def from_partner(array, axis, apart):
    return lax.ppermute(array, axis, [(i, i ^ 1 << apart) for i in range(lax.axis_size(axis))])


def shifted(block, axis, distance):
    devices = range(lax.axis_size(axis))
    route = [(i - distance, i) for i in devices if i - distance in devices]
    return lax.ppermute(block, axis, route)


def anchor(*places):
    return tuple((jnp.asarray(place).astype(jnp.int32) for place in places))


def swap_frames(block):
    return from_partner(block, "tm", 0)


def swap_rowpair(block):
    return from_partner(block, "rows", 0)


def move_time(block, distance):
    return shifted(block, "tm", distance)


def move_rows(block, distance):
    return shifted(block, "rows", distance)


def extend_time(block):
    return jnp.concatenate([move_time(block, 2), block, move_time(block, -2)], axis=1)


def extend_rows(block):
    return jnp.concatenate([move_rows(block, 2), block, move_rows(block, -2)], axis=2)


def pair_join(kept_part, arrived, first_half, axis):
    front = jnp.where(first_half, kept_part, arrived)
    back = jnp.where(first_half, arrived, kept_part)
    return jnp.concatenate([front, back], axis=axis)


def window_allowed(offsets, tile_t, tile_r, row_valid, time_tiles):
    col_tiles = offsets.shape[0]
    step_t = jnp.arange(12, dtype=jnp.int32) // 4 - 1
    key_row = jnp.arange(24, dtype=jnp.int32)
    step_r = key_row // 8 - 1
    row_within = key_row % 8
    step_w = jnp.arange(24, dtype=jnp.int32) // 8 - 1
    time_near = tile_t + step_t
    time_ok = ((time_near >= 0) & (time_near < time_tiles))[None, :] & (
        step_t[None, :] * offsets[:, 0:1] >= 0
    )
    padded = jnp.concatenate([jnp.zeros((1,), jnp.int32), row_valid, jnp.zeros((1,), jnp.int32)])
    nearby_valid = lax.dynamic_slice(padded, anchor(tile_r), (3,))
    picker = step_r[:, None] + 1 == jnp.arange(3, dtype=jnp.int32)[None, :]
    row_limit = jnp.sum(jnp.where(picker, nearby_valid[None, :], 0), axis=1)
    row_ok = (row_within < row_limit)[None, :] & (step_r[None, :] * offsets[:, 1:2] >= 0)
    col_near = jnp.arange(col_tiles, dtype=jnp.int32)[:, None] + step_w[None, :]
    col_ok = (col_near >= 0) & (col_near < col_tiles) & (step_w[None, :] * offsets[:, 2:3] >= 0)
    allowed = time_ok[:, :, None, None] & row_ok[:, None, :, None] & col_ok[:, None, None, :]
    query_ok = jnp.arange(256, dtype=jnp.int32) // 8 % 8 < nearby_valid[1]
    return (allowed.reshape(col_tiles, 6912), query_ok)


def shards(queries, keys, values, win_off, row_valid):
    columns = queries.shape[2]
    channels = queries.shape[3]
    col_tiles = columns // 8
    head_size = HEAD_DIM
    heads_here = channels // 4 // head_size
    time_index = lax.axis_index("tm")
    row_index = lax.axis_index("rows")
    half_t = time_index % 2
    half_r = row_index % 2
    tile_t = time_index // 2
    tile_r = row_index // 2
    time_tiles = lax.axis_size("tm") // 2
    stacked = jnp.stack([queries, keys, values])
    halves = stacked.reshape(3, 2, 4, columns, 2, channels // 2)
    kept_part = lax.dynamic_index_in_dim(halves, half_t, 4, keepdims=False)
    sent_part = lax.dynamic_index_in_dim(halves, 1 - half_t, 4, keepdims=False)
    arrived = swap_frames(sent_part)
    merged = pair_join(kept_part, arrived, half_t == 0, 1)
    halves = merged.reshape(3, 4, 4, columns, 2, channels // 4)
    kept_part = lax.dynamic_index_in_dim(halves, half_r, 4, keepdims=False)
    sent_part = lax.dynamic_index_in_dim(halves, 1 - half_r, 4, keepdims=False)
    arrived = swap_rowpair(sent_part)
    owned_part = pair_join(kept_part, arrived, half_r == 0, 2)
    query_own = owned_part[0]
    key_value = owned_part[1:]
    extended = extend_rows(extend_time(key_value))
    extended = jnp.pad(extended, ((0, 0), (0, 0), (0, 0), (8, 8), (0, 0)))
    query_tiles = query_own.reshape(4, 8, col_tiles, 8, heads_here, head_size)
    query_tiles = jnp.transpose(query_tiles, (2, 0, 1, 3, 4, 5)).reshape(
        col_tiles, 256, heads_here, head_size
    )
    offsets = lax.dynamic_slice(
        win_off, anchor(tile_t, tile_r, 0, 0), (1, 1, col_tiles, 3)
    ).reshape(col_tiles, 3)
    allowed, query_ok = window_allowed(offsets, tile_t, tile_r, row_valid, time_tiles)
    score_scale = 1.0 / head_size**0.5

    def per_head(head):
        head_block = lax.dynamic_slice_in_dim(extended, head * head_size, head_size, axis=4)
        query_head = lax.dynamic_index_in_dim(query_tiles, head, 2, keepdims=False)

        def per_column(column):
            window = lax.dynamic_slice_in_dim(head_block, 8 * column, 24, axis=3).reshape(
                2, 6912, head_size
            )
            query_tile = lax.dynamic_index_in_dim(query_head, column, 0, keepdims=False)
            allow_row = lax.dynamic_index_in_dim(allowed, column, 0, keepdims=False)
            scores = (
                jnp.dot(query_tile, window[0].T, preferred_element_type=jnp.float32) * score_scale
            )
            scores = jnp.where(allow_row[None, :], scores, -jnp.inf)
            row_max = jnp.max(scores, axis=-1, keepdims=True)
            expo = jnp.exp(scores - row_max)
            row_total = jnp.sum(expo, axis=-1)
            weights = expo.astype(jnp.bfloat16)
            summed = jnp.dot(weights, window[1], preferred_element_type=jnp.float32)
            output_tile = summed / row_total[:, None]
            output_tile = jnp.where(query_ok[:, None], output_tile, 0.0)
            return output_tile.astype(jnp.bfloat16)

        return lax.map(per_column, jnp.arange(col_tiles, dtype=jnp.int32))

    results = lax.map(per_head, jnp.arange(heads_here, dtype=jnp.int32))
    output_own = jnp.transpose(results, (1, 2, 0, 3)).reshape(
        col_tiles, 4, 8, 8, heads_here * head_size
    )
    output_own = jnp.transpose(output_own, (1, 2, 0, 3, 4)).reshape(4, 8, columns, channels // 4)
    row_halves = output_own.reshape(4, 2, 4, columns, channels // 4)
    kept_part = lax.dynamic_index_in_dim(row_halves, half_r, 1, keepdims=False)
    sent_part = lax.dynamic_index_in_dim(row_halves, 1 - half_r, 1, keepdims=False)
    arrived = swap_rowpair(sent_part)
    wider_part = pair_join(kept_part, arrived, half_r == 0, 3)
    frame_halves = wider_part.reshape(2, 2, 4, columns, channels // 2)
    kept_part = lax.dynamic_index_in_dim(frame_halves, half_t, 0, keepdims=False)
    sent_part = lax.dynamic_index_in_dim(frame_halves, 1 - half_t, 0, keepdims=False)
    arrived = swap_frames(sent_part)
    return pair_join(kept_part, arrived, half_t == 0, 3)


def solution(mesh):
    return jax.shard_map(
        shards,
        mesh=mesh,
        in_specs=(
            P("tm", "rows", None, None),
            P("tm", "rows", None, None),
            P("tm", "rows", None, None),
            P(),
            P(),
        ),
        out_specs=P("tm", "rows", None, None),
        check_vma=False,
    )
```

profile of v0, /device:TPU:19, one launch (start us, length us, event | category | flops | bytes accessed | tf_op | source)
XLA Modules:
  0.0 799.1 jit_solution(1568711774601438714)
XLA Ops:
  0.0 2.3 stack.12
  2.8 2.9 stack.13
  5.8 2.3 stack.14
  10.4 7.2 constant_dynamic-slice_fusion.7
  19.7 2.8 collective-permute-done
  25.6 4.7 reshape.231
  30.3 6.4 constant_dynamic-slice_fusion.5
  37.0 3.1 collective-permute-start.1
  40.0 51.3 %collective-permute-done.1 = bf16[3,4,4,32,384]{4,3,2,1,0:T(8,128)(2,1)S(1)} collective-permute-done((bf16[3,4,4,32,384]{4,3,2,1,0:T(8,128)(2,1)S(1)}, bf16[3,4,4,32,384]{4,3,2,1,0:T(8,128)(2,1)S(1)}, u32[]{:S(2)}, u32[]{:S(2)}) %collective-permute-start.1) | collective-permute-done | bytes 1179680 | tf_op jit(solution)/shard_map/ppermute | solution.py:10
  92.4 2.4 bitcast_select_fusion
  94.9 3.0 collective-permute-start.2
  98.0 2.4 collective-permute-start.3
  100.4 31.6 %collective-permute-done.2 = bf16[2,4,8,32,384]{4,3,2,1,0:T(8,128)(2,1)S(1)} collective-permute-done((bf16[2,4,8,32,384]{4,3,2,1,0:T(8,128)(2,1)S(1)}, bf16[2,4,8,32,384]{4,3,2,1,0:T(8,128)(2,1)S(1)}, u32[]{:S(2)}, u32[]{:S(2)}) %collective-permute-start.2) | collective-permute-done | bytes 1572896 | tf_op jit(solution)/shard_map/ppermute | solution.py:16
  132.0 2.6 collective-permute-done.3
  134.6 2.6 pad_maximum_fusion
  137.2 8.1 %collective-permute-start.4 = (bf16[2,12,8,32,384]{4,3,2,1,0:T(8,128)(2,1)}, bf16[2,12,8,32,384]{4,3,2,1,0:T(8,128)(2,1)}, u32[]{:S(2)}, u32[]{:S(2)}) collective-permute-start(bf16[2,12,8,32,384]{4,3,2,1,0:T(8,128)(2,1)} %pad_maximum_fusion), channel_id=1, source_target_pairs={{0,2},{1,3},{2,4},{3,5},{4,6},{5,7},{6,8},{7,9},{8,10},{9,11},{10,... | collective-permute-start | bytes 14155784 | tf_op jit(solution)/shard_map/ppermute | solution.py:16
  145.3 2.2 collective-permute-start.5
  151.3 209.9 %collective-permute-done.4 = bf16[2,12,8,32,384]{4,3,2,1,0:T(8,128)(2,1)} collective-permute-done((bf16[2,12,8,32,384]{4,3,2,1,0:T(8,128)(2,1)}, bf16[2,12,8,32,384]{4,3,2,1,0:T(8,128)(2,1)}, u32[]{:S(2)}, u32[]{:S(2)}) %collective-permute-start.4) | collective-permute-done | bytes 4718624 | tf_op jit(solution)/shard_map/ppermute | solution.py:16
  361.2 190.3 %collective-permute-done.5 = bf16[2,12,8,32,384]{4,3,2,1,0:T(8,128)(2,1)} collective-permute-done((bf16[2,12,8,32,384]{4,3,2,1,0:T(8,128)(2,1)}, bf16[2,12,8,32,384]{4,3,2,1,0:T(8,128)(2,1)}, u32[]{:S(2)}, u32[]{:S(2)}) %collective-permute-start.5) | collective-permute-done | bytes 4718624 | tf_op jit(solution)/shard_map/ppermute | solution.py:16
  551.4 22.1 %select_maximum_fusion = bf16[2,12,24,48,384]{4,3,2,1,0:T(8,128)(2,1)} fusion(bf16[2,12,8,32,384]{4,3,2,1,0:T(8,128)(2,1)} %collective-permute-done.5, bf16[2,12,8,32,384]{4,3,2,1,0:T(8,128)(2,1)} %collective-permute-done.4, bf16[2,4,8,32,384]{4,3,2,1,0:T(8,128)(2,1)} %copy-done.6, bf16[2,4,8,32,384]{4,3,2,1,0:T(8,128)(2,1)S(1)} %fusion.36, ...), kind=kLoop, calls=%fused_computation.36 | loop fusion | flops 191102976 | bytes 35389440 | tf_op jit(solution)/shard_map/concatenate | solution.py:44
  574.1 198.8 %while.23 = (s32[]{:T(128)}, bf16[3,4,256,128]{3,2,1,0:T(8,128)(2,1)}, s32[3]{0:T(128)}, bf16[2,12,24,48,384]{4,3,2,1,0:T(8,128)(2,1)}, bf16[4,256,3,128]{3,1,0,...) while((s32[]{:T(128)}, ...), condition=%wide.region_6.7_spmd.clone, body=%wide.region_1.6_spmd.clone.sunk | while | flops 918486528 | bytes 47298152 | solution.py:139
  576.1 7.8 constant_dynamic-slice_fusion.10
  590.0 48.6 %while.24 = (s32[]{:T(128)}, bf16[4,256,128]{2,1,0:T(8,128)(2,1)}, pred[256]{0:T(512)(128)(4,1)S(1)}, s32[4]{0:T(128)}, pred[4,6912]{1,0:T(4,128)(4,1)}, /*index...) while((s32[]{:T(128)}, bf16[4,256,128]{2,1,0:T(8,128)(2,1)}, ...), condition=%wide.region_5.5_spmd, body=%wide.region_2.4_spmd.sunk | while | flops 918453760 | bytes 32008436 | solution.py:137
  591.8 2.7 constant_dynamic-slice_fusion.11
  597.0 2.0 fusion.60
  604.0 2.7 constant_dynamic-slice_fusion.11
  616.1 2.7 constant_dynamic-slice_fusion.11
  621.3 2.0 fusion.60
  628.3 2.7 constant_dynamic-slice_fusion.11
  642.3 7.8 constant_dynamic-slice_fusion.10
  656.3 48.6 %while.24 = (s32[]{:T(128)}, bf16[4,256,128]{2,1,0:T(8,128)(2,1)}, pred[256]{0:T(512)(128)(4,1)S(1)}, s32[4]{0:T(128)}, pred[4,6912]{1,0:T(4,128)(4,1)}, /*index...) while((s32[]{:T(128)}, bf16[4,256,128]{2,1,0:T(8,128)(2,1)}, ...), condition=%wide.region_5.5_spmd, body=%wide.region_2.4_spmd.sunk | while | flops 918453760 | bytes 32008436 | solution.py:137
  658.1 2.7 constant_dynamic-slice_fusion.11
  663.3 2.0 fusion.60
  670.3 2.7 constant_dynamic-slice_fusion.11
  682.4 2.7 constant_dynamic-slice_fusion.11
  687.7 2.0 fusion.60
  694.6 2.7 constant_dynamic-slice_fusion.11
  699.8 2.0 fusion.60
  708.6 7.8 constant_dynamic-slice_fusion.10
  722.6 48.6 %while.24 = (s32[]{:T(128)}, bf16[4,256,128]{2,1,0:T(8,128)(2,1)}, pred[256]{0:T(512)(128)(4,1)S(1)}, s32[4]{0:T(128)}, pred[4,6912]{1,0:T(4,128)(4,1)}, /*index...) while((s32[]{:T(128)}, bf16[4,256,128]{2,1,0:T(8,128)(2,1)}, ...), condition=%wide.region_5.5_spmd, body=%wide.region_2.4_spmd.sunk | while | flops 918453760 | bytes 32008436 | solution.py:137
  724.4 2.7 constant_dynamic-slice_fusion.11
  736.5 2.7 constant_dynamic-slice_fusion.11
  741.7 2.0 fusion.60
  748.7 2.7 constant_dynamic-slice_fusion.11
  753.9 2.0 fusion.60
  760.8 2.7 constant_dynamic-slice_fusion.11
  766.1 2.0 fusion.60
  775.6 18.9 %collective-permute-done.6 = bf16[4,4,32,384]{3,2,1,0:T(8,128)(2,1)S(1)} collective-permute-done((bf16[4,4,32,384]{3,2,1,0:T(8,128)(2,1)S(1)}, bf16[4,4,32,384]{3,2,1,0:T(8,128)(2,1)S(1)}, u32[]{:S(2)}, u32[]{:S(2)}) %collective-permute-start.6) | collective-permute-done | bytes 393248 | tf_op jit(solution)/shard_map/ppermute | solution.py:10
  (133 shorter events, 112.7 us)
Async XLA Ops:
  0.0 147.6 %copy-start = (s32[8,8,4,3]{1,2,3,0:T(4,128)S(1)}, s32[8,8,4,3]{1,2,3,0:T(4,128)}, u32[]{:S(2)}) copy-start(s32[8,8,4,3]{1,2,3,0:T(4,128)} %param.12) | copy-start | bytes 9220
  17.7 4.8 copy-start.3
  19.0 3.5 collective-permute-start
  37.0 54.4 %collective-permute-start.1 = (bf16[3,4,4,32,384]{4,3,2,1,0:T(8,128)(2,1)S(1)}, bf16[3,4,4,32,384]{4,3,2,1,0:T(8,128)(2,1)S(1)}, u32[]{:S(2)}, u32[]{:S(2)}) collective-permute-start(bf16[3,4,4,32,384]{4,3,2,1,0:T(8,128)(2,1)S(1)} %bitcast.90), channel_id=1, source_target_pairs={{0,1},{1,0},{2,3},{3,2},{4,5},{5,4},{6,7},{7,6},{8,9},{9,8},{10,11... | collective-permute-start | bytes 3538952 | tf_op jit(solution)/shard_map/ppermute | solution.py:10
  91.4 1.0 copy-start.7
  94.7 37.3 %copy-start.2 = (bf16[3,4,4,32,384]{4,3,2,1,0:T(8,128)(2,1)}, bf16[3,4,4,32,384]{4,3,2,1,0:T(8,128)(2,1)S(1)}, u32[]{:S(2)}) copy-start(bf16[3,4,4,32,384]{4,3,2,1,0:T(8,128)(2,1)S(1)} %get-tuple-element.141) | copy-start | bytes 3538948
  94.9 52.9 %copy-start.8 = (s32[8]{0:T(128)S(1)}, s32[8]{0:T(128)}, u32[]{:S(2)}) copy-start(s32[8]{0:T(128)} %param.13) | copy-start | bytes 100
  94.9 37.1 %collective-permute-start.2 = (bf16[2,4,8,32,384]{4,3,2,1,0:T(8,128)(2,1)S(1)}, bf16[2,4,8,32,384]{4,3,2,1,0:T(8,128)(2,1)S(1)}, u32[]{:S(2)}, u32[]{:S(2)}) collective-permute-start(bf16[2,4,8,32,384]{4,3,2,1,0:T(8,128)(2,1)S(1)} %fusion.36), channel_id=1, source_target_pairs={{0,32},{16,48},{32,64},{48,80},{64,96},{80,112},{96,128},{112,144}... | collective-permute-start | bytes 4718600 | tf_op jit(solution)/shard_map/ppermute | solution.py:16
  98.0 36.6 %collective-permute-start.3 = (bf16[2,4,8,32,384]{4,3,2,1,0:T(8,128)(2,1)S(1)}, bf16[2,4,8,32,384]{4,3,2,1,0:T(8,128)(2,1)S(1)}, u32[]{:S(2)}, u32[]{:S(2)}) collective-permute-start(bf16[2,4,8,32,384]{4,3,2,1,0:T(8,128)(2,1)S(1)} %fusion.36), channel_id=1, source_target_pairs={{32,0},{48,16},{64,32},{80,48},{96,64},{112,80},{128,96},{144,112}... | collective-permute-start | bytes 4718600 | tf_op jit(solution)/shard_map/ppermute | solution.py:16
  132.0 5.2 copy-start.4
  134.6 2.6 copy-start.6
  137.2 224.0 %collective-permute-start.4 = (bf16[2,12,8,32,384]{4,3,2,1,0:T(8,128)(2,1)}, bf16[2,12,8,32,384]{4,3,2,1,0:T(8,128)(2,1)}, u32[]{:S(2)}, u32[]{:S(2)}) collective-permute-start(bf16[2,12,8,32,384]{4,3,2,1,0:T(8,128)(2,1)} %pad_maximum_fusion), channel_id=1, source_target_pairs={{0,2},{1,3},{2,4},{3,5},{4,6},{5,7},{6,8},{7,9},{8,10},{9,11},{10,... | collective-permute-start | bytes 14155784 | tf_op jit(solution)/shard_map/ppermute | solution.py:16
  145.3 406.1 %collective-permute-start.5 = (bf16[2,12,8,32,384]{4,3,2,1,0:T(8,128)(2,1)}, bf16[2,12,8,32,384]{4,3,2,1,0:T(8,128)(2,1)}, u32[]{:S(2)}, u32[]{:S(2)}) collective-permute-start(bf16[2,12,8,32,384]{4,3,2,1,0:T(8,128)(2,1)} %pad_maximum_fusion), channel_id=1, source_target_pairs={{2,0},{3,1},{4,2},{5,3},{6,4},{7,5},{8,6},{9,7},{10,8},{11,9},{12,... | collective-permute-start | bytes 14155784 | tf_op jit(solution)/shard_map/ppermute | solution.py:16
  150.2 401.3 %copy-start.5 = (bf16[2,4,8,32,384]{4,3,2,1,0:T(8,128)(2,1)S(1)}, bf16[2,4,8,32,384]{4,3,2,1,0:T(8,128)(2,1)}, u32[]{:S(2)}) copy-start(bf16[2,4,8,32,384]{4,3,2,1,0:T(8,128)(2,1)} %copy-done.4) | copy-start | bytes 4718596
  775.5 19.0 %collective-permute-start.6 = (bf16[4,4,32,384]{3,2,1,0:T(8,128)(2,1)S(1)}, bf16[4,4,32,384]{3,2,1,0:T(8,128)(2,1)S(1)}, u32[]{:S(2)}, u32[]{:S(2)}) collective-permute-start(bf16[4,4,32,384]{3,2,1,0:T(8,128)(2,1)S(1)} %dynamic-slice_bitcast_fusion.2), channel_id=1, source_target_pairs={{0,1},{1,0},{2,3},{3,2},{4,5},{5,4},{6,7},{7,6},{8,9},{9,8},{10,11... | collective-permute-start | bytes 1179656 | tf_op jit(solution)/shard_map/ppermute | solution.py:10
  794.6 4.5 copy-start.1
  794.8 3.4 collective-permute-start.7
where the time goes:
time: 802 us; the launch traced here: 799 us
  waiting for transfers between devices  509 us (63%)
  local copies, waits for them, and re-layouts  136 us (17%)
  other arithmetic  49.2 us (6%)
  matrix products  47.8 us (6%)
  loops' own time  35.4 us (4%)
  starting transfers between devices  21.6 us (3%)
    ppermute x4, waiting for transfers between devices, shifted(): return lax.ppermute(block, axis, route)  434 us
    ppermute x4, waiting for transfers between devices, from_partner(): lax.ppermute(array, axis, [(i, i ^ 1 << apart) for i in range(lax.axis_si...  74.4 us
    slice x12, local copies, waits for them, and re-layouts, per_column(): window[0]  32.1 us
    another operation x3, loops' own time, per_head(): return lax.map(per_column, jnp.arange(col_tiles, dtype=jnp.int32))  27.1 us
    dot_general x12, matrix products, per_column(): jnp.dot(query_tile, window[0].T, preferred_element_type=jnp.float32)  24.2 us
    dot_general x12, matrix products, per_column(): summed = jnp.dot(weights, window[1], preferred_element_type=jnp.float32)  23.6 us
    dynamic_slice x3, local copies, waits for them, and re-layouts, per_head(): lax.dynamic_slice_in_dim(extended, head * head_size, head_size, axis=4)  23.4 us
    concatenate x1, other arithmetic, extend_rows(): jnp.concatenate([move_rows(block, 2), block, move_rows(block, -2)], axis=2)  22.1 us
  transfers between devices with their start and end apart: 8, of which 8 were waited for; matrix products, arithmetic and copies ran while one was open for 0% of the time, Pallas kernels for 0%

commit v1 on v0

v1 whole, which is shorter than its diff:
```python
import jax
import jax.numpy as jnp
from jax import lax
from jax.experimental import pallas as pl
from jax.experimental.pallas import tpu as pltpu
from jax.sharding import PartitionSpec as P

HEADS = 12
HEAD_DIM = 128
LOG2E = 1.4426950408889634
SCALE = LOG2E / HEAD_DIM**0.5
BF16 = jnp.bfloat16
F32 = jnp.float32
MESH = pl.DeviceIdType.MESH
VMEM_LIMIT = 60 * 1024 * 1024


def rem(a, b):
    return lax.rem(a, jnp.int32(b))


def div(a, b):
    return lax.div(a, jnp.int32(b))


class Place:
    def __init__(self):
        tm = lax.axis_index("tm")
        rows = lax.axis_index("rows")
        self.zl = div(tm, 8)
        self.y = rem(div(tm, 2), 4)
        self.core = rem(tm, 2)
        self.x = div(rows, 4)
        self.zh = rem(rows, 4)
        self.zz = div(self.zh, 2)
        self.zp = rem(self.zh, 2)
        self.z = self.zh * 2 + self.zl
        self.t = self.core * 4 + self.y
        self.rows = rows

    def worker(self, k):
        z = rem(self.z + k, 8)
        zh, zl = div(z, 2), rem(z, 2)
        return zh, zl, (zl * 8 + self.y * 2 + self.zl, self.x * 4 + zh)

    def origin(self, k):
        i = rem(self.z + k, 8)
        zh = rem(self.zh + k // 2, 4)
        core = rem(self.core + k % 2, 2)
        return zh, core, (self.core * 8 + self.y * 2 + core, self.x * 4 + zh)

    def time_neighbour(self, step):
        t = self.t + step
        ok = (t >= 0) & (t < 8)
        t = jnp.clip(t, 0, 7)
        return ok, (self.zl * 8 + rem(t, 4) * 2 + div(t, 4), self.rows)

    def row_neighbour(self, step):
        x = self.x + step
        ok = (x >= 0) & (x < 4)
        x = jnp.clip(x, 0, 3)
        return ok, (self.zl * 8 + self.y * 2 + self.core, x * 4 + self.zh)


CHUNKS = ((0, 0, 4), (1, 0, 4), (0, 4, 3), (1, 4, 3))


def gather_kernel(q_in, k_in, v_in, kv, qs, packed, send_kv, send_y, send_x, recv_kv, recv_q, recv_y, recv_x):
    me = Place()
    times = [me.time_neighbour(s) for s in (1, -1)]
    sides = [me.row_neighbour(s) for s in (1, -1)]
    myself = me.core == me.zl

    barrier = pltpu.get_barrier_semaphore()
    expect = jnp.int32(0)
    for k in range(8):
        _, _, device = me.origin(k)
        if k == 0:
            @pl.when(jnp.logical_not(myself))
            def _():
                pl.semaphore_signal(barrier, inc=1, device_id=device, device_id_type=MESH)
        else:
            pl.semaphore_signal(barrier, inc=1, device_id=device, device_id_type=MESH)
    for ok, device in times + sides:
        @pl.when(ok)
        def _():
            pl.semaphore_signal(barrier, inc=1, device_id=device, device_id_type=MESH)
        expect = expect + ok.astype(jnp.int32)

    def pack(which, source):
        for h in range(HEADS):
            block = source[:, :, :, h * HEAD_DIM:(h + 1) * HEAD_DIM].astype(F32)
            block = block.reshape(2, 4, 4, 8, HEAD_DIM)
            block = jnp.transpose(block, (2, 1, 0, 3, 4)).reshape(4, 4, 16, HEAD_DIM)
            packed[which, h] = block.astype(BF16)

    def spread(which, first, count, recv):
        index = which * 2 + (first > 0)
        for k in range(8):
            zh, zl, device = me.worker(k)
            if first == 0:
                head, column = 3 * zh + 2 * zl, 0
            else:
                head, column = 3 * zh + 1, (2 * zl if which == 2 else zl)
            source = packed.at[which, head, pl.ds(column, count)]
            slots, rows, spot = pl.ds(first, count), pl.ds(me.zp * 4, 4), pl.ds(pl.multiple_of(me.core * 16, 16), 16)
            if which == 2:
                target = qs.at[me.zz, slots, rows, spot]
            else:
                target = kv.at[which, 1, 1 + me.zz, slots, rows, spot]
            remote = pltpu.make_async_remote_copy(
                source, target, send_kv.at[index, k], recv, device_id=device, device_id_type=MESH)
            if k == 0:
                @pl.when(myself)
                def _():
                    pltpu.make_async_copy(source, target, recv).start()

                @pl.when(jnp.logical_not(myself))
                def _():
                    remote.start()
            else:
                remote.start()

    def spread_done(which, first, count):
        index = which * 2 + (first > 0)
        source = packed.at[which, 0, pl.ds(0, count)]
        for k in range(8):
            def done():
                pltpu.make_async_copy(source, source, send_kv.at[index, k]).wait()
            if k == 0:
                pl.when(jnp.logical_not(myself))(done)
            else:
                done()

    def y_copy(c, d):
        which, first, count = CHUNKS[c]
        source = kv.at[which, 1, pl.ds(1, 2), pl.ds(first, count)]
        target = kv.at[which, 2 * d, pl.ds(1, 2), pl.ds(first, count)]
        return pltpu.make_async_remote_copy(
            source, target, send_y.at[c, d], recv_y.at[c, d], device_id=times[d][1], device_id_type=MESH)

    def x_copy(c, d, dt):
        which, first, count = CHUNKS[c]
        source = kv.at[which, dt, 2 - d, pl.ds(first, count)]
        target = kv.at[which, dt, 3 * d, pl.ds(first, count)]
        return pltpu.make_async_remote_copy(
            source, target, send_x.at[c, d, dt], recv_x.at[c, d, dt], device_id=sides[d][1], device_id_type=MESH)

    has_time = [times[1][0], times[0][0], None]

    def dt_ok(dt):
        return {0: times[1][0], 1: True, 2: times[0][0]}[dt]

    def send_x_part(c, dt):
        for d in range(2):
            @pl.when(sides[d][0] & dt_ok(dt))
            def _():
                x_copy(c, d, dt).start()

    def after_y(c):
        for d in range(2):
            @pl.when(times[1 - d][0])
            def _():
                y_copy(c, d).wait_recv()
            send_x_part(c, 2 * d)

    pack(0, k_in)
    pl.semaphore_wait(barrier, expect + 8 - myself.astype(jnp.int32))
    spread(0, 0, 4, recv_kv.at[0])
    pack(1, v_in)
    spread(1, 0, 4, recv_kv.at[1])
    spread(0, 4, 3, recv_kv.at[2])
    spread(1, 4, 3, recv_kv.at[3])
    pack(2, q_in)
    spread(2, 0, 4, recv_q.at[0])
    spread(2, 4, 2, recv_q.at[1])
    for c in range(4):
        which, first, count = CHUNKS[c]
        whole = kv.at[which, 1, pl.ds(1, 2), pl.ds(first, count)]
        pltpu.make_async_copy(whole, whole, recv_kv.at[c]).wait()
        for d in range(2):
            @pl.when(times[d][0])
            def _():
                y_copy(c, d).start()
        send_x_part(c, 1)
        if c:
            after_y(c - 1)
    after_y(3)
    for i, (first, count) in enumerate(((0, 4), (4, 2))):
        whole = qs.at[:, pl.ds(first, count)]
        pltpu.make_async_copy(whole, whole, recv_q.at[i]).wait()
    for c in range(4):
        for d in range(2):
            for dt in range(3):
                @pl.when(sides[1 - d][0] & dt_ok(dt))
                def _():
                    x_copy(c, d, dt).wait_recv()
    for c in range(4):
        for d in range(2):
            @pl.when(times[d][0])
            def _():
                y_copy(c, d).wait_send()
            for dt in range(3):
                @pl.when(sides[d][0] & dt_ok(dt))
                def _():
                    x_copy(c, d, dt).wait_send()
    for which in range(3):
        spread_done(which, 0, 4)
        spread_done(which, 4, 2 if which == 2 else 3)


def attend_kernel(offsets, row_valid, kv, qs, out, turned, scores, top, total, gathered):
    me = Place()

    def turn(i, _):
        dt, row = div(i, 4), rem(i, 4)
        for c in range(7):
            turned[dt, row, c] = kv[1, dt, row, c].reshape(256, HEAD_DIM).astype(F32).T.astype(BF16)
        return 0

    lax.fori_loop(0, 12, turn, 0)

    def limit(row):
        tile = 2 * me.x - 1 + row
        inside = (tile >= 0) & (tile < 8)
        return jnp.where(inside, row_valid[jnp.clip(tile, 0, 7)], 0)

    row_number = lax.broadcasted_iota(jnp.int32, (8, 1, 256), 0)

    def tile(r, slot, base, count, column, first):
        flat = ((me.t * 8 + 2 * me.x + r) * 4 + column) * 3
        off_t, off_r, off_c = offsets[flat], offsets[flat + 1], offsets[flat + 2]
        query = qs[r, slot].reshape(256, HEAD_DIM)
        top[...] = jnp.full((8, 256), -jnp.inf, F32)
        total[...] = jnp.zeros((8, 256), F32)
        gathered[...] = jnp.zeros((HEAD_DIM, 256), F32)

        def near(b):
            dt, dr = div(b, 3), rem(b, 3)
            when = me.t + dt - 1
            ok = (when >= 0) & (when < 8) & ((dt - 1) * off_t >= 0) & ((dr - 1) * off_r >= 0)
            valid = jnp.where(ok, limit(r + dr), 0)
            valids = [jnp.where((first + j) * off_c >= 0, valid, 0) for j in range(count)]
            return dt, r + dr, valid, valids

        def score(b, _):
            dt, row, valid, valids = near(b)

            @pl.when(valid > 0)
            def _():
                keys = kv[0, dt, row, pl.ds(base, count)].reshape(count * 256, HEAD_DIM)
                s = lax.dot_general(keys, query, (((1,), (1,)), ((), ())), preferred_element_type=F32)
                scores[b, pl.ds(0, count * 256)] = s
                best = jnp.max(s.reshape(count, 8, 4, 8, 256), axis=2)
                for j in range(count):
                    mine = jnp.where(row_number < valids[j], best[j], -jnp.inf)
                    top[...] = jnp.maximum(top[...], jnp.max(mine, axis=0))
            return 0

        lax.fori_loop(0, 9, score, 0)
        shift = jnp.max(top[...], axis=0, keepdims=True) * SCALE

        def weigh(b, _):
            dt, row, valid, valids = near(b)

            @pl.when(valid > 0)
            def _():
                for j in range(count):
                    s = scores[b, pl.ds(j * 256, 256)].reshape(8, 32, 256)
                    less = jnp.where(row_number < valids[j], shift[None], jnp.inf)
                    p = jnp.exp2(s * SCALE - less)
                    total[...] += jnp.sum(p.reshape(32, 8, 256), axis=0)
                    weights = p.reshape(256, 256).astype(BF16)
                    gathered[...] += jnp.dot(turned[dt, row, base + j], weights, preferred_element_type=F32)
            return 0

        lax.fori_loop(0, 9, weigh, 0)
        result = gathered[...] / jnp.sum(total[...], axis=0, keepdims=True)
        result = result.T.reshape(8, 32, HEAD_DIM)
        keep = lax.broadcasted_iota(jnp.int32, (8, 1, HEAD_DIM), 0) < limit(r + 1)
        out[r, slot] = jnp.where(keep, result, 0.0).astype(BF16)

    def wide(i, _):
        r, kind = div(i, 3), rem(i, 3)
        shared = kind == 2
        slot = jnp.where(shared, 5 - me.zl, 1 + kind)
        base = jnp.where(shared, 4, kind)
        column = jnp.where(shared, 1 + me.zl, 1 + kind)
        tile(r, slot, base, 3, column, -1)
        return 0

    def edge(i, _):
        r, kind = div(i, 3), rem(i, 3)
        shared = kind == 2
        right = jnp.where(shared, me.zl, kind)
        slot = jnp.where(shared, 4 + me.zl, 3 * kind)
        base = jnp.where(shared, 4 + me.zl, 2 * kind)
        tile(r, slot, base, 2, 3 * right, -right)
        return 0

    lax.fori_loop(0, 6, wide, 0)
    lax.fori_loop(0, 6, edge, 0)


def return_kernel(tiles, out, landed, send, recv):
    me = Place()
    myself = me.core == me.zl
    barrier = pltpu.get_barrier_semaphore()
    for k in range(8):
        _, _, device = me.worker(k)
        if k == 0:
            @pl.when(jnp.logical_not(myself))
            def _():
                pl.semaphore_signal(barrier, inc=1, device_id=device, device_id_type=MESH)
        else:
            pl.semaphore_signal(barrier, inc=1, device_id=device, device_id_type=MESH)
    pl.semaphore_wait(barrier, 8 - myself.astype(jnp.int32))

    def copies(k, part):
        zh, core, device = me.origin(k)
        rows, spot = pl.ds(rem(zh, 2) * 4, 4), pl.ds(pl.multiple_of(core * 16, 16), 16)
        if part == 0:
            source = tiles.at[div(zh, 2), pl.ds(0, 4), rows, spot]
            target = landed.at[3 * me.zh + 2 * me.zl]
        else:
            source = tiles.at[div(zh, 2), pl.ds(4, 2), rows, spot]
            target = landed.at[3 * me.zh + 1, pl.ds(2 * me.zl, 2)]
        return source, target, pltpu.make_async_remote_copy(
            source, target, send.at[part, k], recv.at[0], device_id=device, device_id_type=MESH)

    for part in range(2):
        for k in range(8):
            source, target, remote = copies(k, part)
            if k == 0:
                @pl.when(myself)
                def _():
                    pltpu.make_async_copy(source, target, recv.at[0]).start()

                @pl.when(jnp.logical_not(myself))
                def _():
                    remote.start()
            else:
                remote.start()
    pltpu.make_async_copy(landed, landed, recv.at[0]).wait()
    for h in range(HEADS):
        block = landed[h].astype(F32).reshape(4, 4, 2, 8, HEAD_DIM)
        block = jnp.transpose(block, (2, 1, 0, 3, 4)).reshape(2, 4, 32, HEAD_DIM)
        out[:, :, :, h * HEAD_DIM:(h + 1) * HEAD_DIM] = block.astype(BF16)
    for part in range(2):
        for k in range(8):
            def done():
                copies(k, part)[2].wait_send()
            if k == 0:
                pl.when(jnp.logical_not(myself))(done)
            else:
                done()


def vmem():
    return pl.BlockSpec(memory_space=pltpu.VMEM)


def anywhere():
    return pl.BlockSpec(memory_space=pl.ANY)


def smem():
    return pl.BlockSpec(memory_space=pltpu.SMEM)


def shards(queries, keys, values, win_off, row_valid):
    dma = pltpu.SemaphoreType.DMA
    kv, qs = pl.pallas_call(
        gather_kernel,
        out_shape=(
            jax.ShapeDtypeStruct((2, 3, 4, 7, 8, 32, HEAD_DIM), BF16),
            jax.ShapeDtypeStruct((2, 6, 8, 32, HEAD_DIM), BF16),
        ),
        in_specs=[vmem()] * 3,
        out_specs=(anywhere(), anywhere()),
        scratch_shapes=[
            pltpu.VMEM((3, HEADS, 4, 4, 16, HEAD_DIM), BF16),
            dma((6, 8)), dma((4, 2)), dma((4, 2, 3)),
            dma((4,)), dma((2,)), dma((4, 2)), dma((4, 2, 3)),
        ],
        compiler_params=pltpu.CompilerParams(
            collective_id=0, has_side_effects=True, vmem_limit_bytes=VMEM_LIMIT),
    )(queries, keys, values)
    tiles = pl.pallas_call(
        attend_kernel,
        out_shape=jax.ShapeDtypeStruct((2, 6, 8, 32, HEAD_DIM), BF16),
        in_specs=[smem(), smem(), vmem(), vmem()],
        out_specs=vmem(),
        scratch_shapes=[
            pltpu.VMEM((3, 4, 7, HEAD_DIM, 256), BF16),
            pltpu.VMEM((9, 768, 256), F32),
            pltpu.VMEM((8, 256), F32),
            pltpu.VMEM((8, 256), F32),
            pltpu.VMEM((HEAD_DIM, 256), F32),
        ],
        compiler_params=pltpu.CompilerParams(vmem_limit_bytes=VMEM_LIMIT),
    )(win_off.reshape(-1), row_valid, kv, qs)
    return pl.pallas_call(
        return_kernel,
        out_shape=jax.ShapeDtypeStruct(queries.shape, BF16),
        in_specs=[anywhere()],
        out_specs=vmem(),
        scratch_shapes=[
            pltpu.VMEM((HEADS, 4, 4, 16, HEAD_DIM), BF16),
            dma((2, 8)), dma((1,)),
        ],
        compiler_params=pltpu.CompilerParams(
            collective_id=1, has_side_effects=True, vmem_limit_bytes=VMEM_LIMIT),
    )(tiles)


def solution(mesh):
    return jax.shard_map(
        shards,
        mesh=mesh,
        in_specs=(
            P("tm", "rows", None, None),
            P("tm", "rows", None, None),
            P("tm", "rows", None, None),
            P(),
            P(),
        ),
        out_specs=P("tm", "rows", None, None),
        check_vma=False,
    )
```

time: 802 us -> 171 us (0.21)
  waiting for transfers between devices: 509 us -> 0 us
  Pallas kernels: 0 us -> 165 us
  local copies, waits for them, and re-layouts: 136 us -> 3.93 us
  other arithmetic: 49.2 us -> 0 us
  matrix products: 47.8 us -> 0 us
  loops' own time: 35.4 us -> 0 us
  starting transfers between devices: 21.6 us -> 0 us
    ppermute x8 -> x0, waiting for transfers between devices: 509 us -> none  [the longest x4 434 us: shifted(): return lax.ppermute(block, axis, route)]
    pallas_call x0 -> x3, Pallas kernels: none -> 165 us  [the longest x1 90.8 us: shards(): pl.pallas_call(gather_kernel, out_shape=(jax.ShapeDtypeStruct((2, 3, 4, 7...]
    dynamic_slice x35 -> x0, local copies, waits for them, and re-layouts: 66.4 us -> none  [the longest x3 23.4 us: per_head(): lax.dynamic_slice_in_dim(extended, head * head_size, head_size, axis=4)]
    dot_general x24 -> x0, matrix products: 47.8 us -> none  [the longest x12 24.2 us: per_column(): jnp.dot(query_tile, window[0].T, preferred_element_type=jnp.float32)]
    another operation x4 -> x0, loops' own time: 35.4 us -> none  [the longest x3 27.1 us: per_head(): return lax.map(per_column, jnp.arange(col_tiles, dtype=jnp.int32))]
    slice x14 -> x0, local copies, waits for them, and re-layouts: 32.9 us -> none  [the longest x12 32.1 us: per_column(): window[0]]
    concatenate x7 -> x0, other arithmetic: 27.6 us -> none  [the longest x1 22.1 us: extend_rows(): jnp.concatenate([move_rows(block, 2), block, move_rows(block, -2)], axis=2)]
    ppermute x8 -> x0, starting transfers between devices: 21.6 us -> none  [the longest x4 15.7 us: shifted(): return lax.ppermute(block, axis, route)]
  transfers between devices with their start and end apart: 8 -> 0, of which waited for: 8 -> 0; matrix products, arithmetic and copies ran while one was open for 0% -> 0% of each run, Pallas kernels for 0% -> 0%
where the time goes in v1:
time: 171 us; the launch traced here: 169 us
  Pallas kernels  165 us (96%)
  local copies, waits for them, and re-layouts  3.93 us (2%)
    pallas_call x1, Pallas kernels, shards(): pl.pallas_call(gather_kernel, out_shape=(jax.ShapeDtypeStruct((2, 3, 4, 7...  90.8 us
    pallas_call x1, Pallas kernels, shards(): pl.pallas_call(attend_kernel, out_shape=jax.ShapeDtypeStruct((2, 6, 8, 32...  53.4 us
    pallas_call x1, Pallas kernels, shards(): pl.pallas_call(return_kernel, out_shape=jax.ShapeDtypeStruct(queries.shap...  21 us

profile of v1, /device:TPU:19, one launch (start us, length us, event | category | flops | bytes accessed | tf_op | source)
XLA Modules:
  0.0 169.1 jit_solution(17304191312554663824)
XLA Ops:
  0.0 1.1 copy.6
  1.1 0.8 reshape.3.offsets
  1.9 90.8 %shard_map.55 = (bf16[2,3,4,7,8,32,128]{6,5,4,3,2,1,0:T(8,128)(2,1)}, bf16[2,6,8,32,128]{4,3,2,1,0:T(8,128)(2,1)}) custom-call(bf16[2,4,32,1536]{3,2,1,0:T(8,128)(2,1)} %q_in.1, bf16[2,4,32,1536]{3,2,1,0:T(8,128)(2,1)} %k_in.1, bf16[2,4,32,1536]{3,2,1,0:T(8,128)(2,1)} %v_in.1), custom_call_target="tpu_custom_call" | custom-call | tf_op jit(solution)/shard_map/pallas_call | solution.py:373
  92.6 53.4 %shard_map.56.tiles = bf16[2,6,8,32,128]{4,3,2,1,0:T(8,128)(2,1)} custom-call(s32[768]{0:T(1024)} %reshape.3.offsets, s32[8]{0:T(128)} %row_valid.1, bf16[2,3,4,7,8,32,128]{6,5,4,3,2,1,0:T(8,128)(2,1)} %get-tuple-element.7.kv, bf16[2,6,8,32,128]{4,3,2,1,0:T(8,128)(2,1)} %get-tuple-element.8.qs), custom_call_target="tpu_custom_call" | custom-call | tf_op jit(solution)/shard_map/pallas_call | solution.py:389
  146.0 21.0 %shard_map.57 = bf16[2,4,32,1536]{3,2,1,0:T(8,128)(2,1)} custom-call(bf16[2,6,8,32,128]{4,3,2,1,0:T(8,128)(2,1)} %shard_map.56.tiles), custom_call_target="tpu_custom_call" | custom-call | tf_op jit(solution)/shard_map/pallas_call | solution.py:403
  167.1 2.1 %copy.8 = bf16[2,4,32,1536]{3,2,1,0:T(8,128)(2,1)} copy(bf16[2,4,32,1536]{3,2,1,0:T(8,128)(2,1)} %shard_map.57) | data formatting | bytes 1572864

commit v2 on v0

v2 whole, which is shorter than its diff:
```python
import jax
import jax.numpy as jnp
from jax import lax
from jax.experimental import pallas as pl
from jax.experimental.pallas import tpu as pltpu
from jax.sharding import PartitionSpec as P

HEADS = 12
HEAD_DIM = 128
LOG2E = 1.4426950408889634
SCALE = LOG2E / HEAD_DIM**0.5
BF16 = jnp.bfloat16
F32 = jnp.float32
MESH = pl.DeviceIdType.MESH
VMEM_LIMIT = 60 * 1024 * 1024


def rem(a, b):
    return lax.rem(a, jnp.int32(b))


def div(a, b):
    return lax.div(a, jnp.int32(b))


class Place:
    def __init__(self):
        tm = lax.axis_index("tm")
        rows = lax.axis_index("rows")
        self.zl = div(tm, 8)
        self.y = rem(div(tm, 2), 4)
        self.core = rem(tm, 2)
        self.x = div(rows, 4)
        self.zh = rem(rows, 4)
        self.zz = div(self.zh, 2)
        self.zp = rem(self.zh, 2)
        self.z = self.zh * 2 + self.zl
        self.t = self.core * 4 + self.y
        self.rows = rows

    def worker(self, k):
        z = rem(self.z + k, 8)
        zh, zl = div(z, 2), rem(z, 2)
        return zh, zl, (zl * 8 + self.y * 2 + self.zl, self.x * 4 + zh)

    def origin(self, k):
        i = rem(self.z + k, 8)
        zh = rem(self.zh + k // 2, 4)
        core = rem(self.core + k % 2, 2)
        return zh, core, (self.core * 8 + self.y * 2 + core, self.x * 4 + zh)

    def time_neighbour(self, step):
        t = self.t + step
        ok = (t >= 0) & (t < 8)
        t = jnp.clip(t, 0, 7)
        return ok, (self.zl * 8 + rem(t, 4) * 2 + div(t, 4), self.rows)

    def row_neighbour(self, step):
        x = self.x + step
        ok = (x >= 0) & (x < 4)
        x = jnp.clip(x, 0, 3)
        return ok, (self.zl * 8 + self.y * 2 + self.core, x * 4 + self.zh)


GROUPS = ((0, 2), (2, 2), (4, 3))
CHUNKS = tuple((which, first, count) for first, count in GROUPS for which in (0, 1))
QUERY_GROUPS = ((0, 4), (4, 2))


def kernel(offsets, row_valid, q_in, k_in, v_in, out, kv, qs, packed, tiles, landed, scores, top, total, gathered,
           send_kv, send_q, send_y, send_x, send_o, recv_kv, recv_q, recv_y, recv_x, recv_o):
    me = Place()
    times = [me.time_neighbour(s) for s in (1, -1)]
    sides = [me.row_neighbour(s) for s in (1, -1)]
    myself = me.core == me.zl
    other = jnp.logical_not(myself)

    for i, dt in ((1, 0), (0, 2)):
        @pl.when(jnp.logical_not(times[i][0]))
        def _():
            kv[:, dt] = jnp.zeros((2, 4, 7, 8, 32, HEAD_DIM), BF16)
    for i, row in ((1, 0), (0, 3)):
        @pl.when(jnp.logical_not(sides[i][0]))
        def _():
            kv[:, :, row] = jnp.zeros((2, 3, 7, 8, 32, HEAD_DIM), BF16)

    barrier = pltpu.get_barrier_semaphore()

    def greet(device):
        pl.semaphore_signal(barrier, inc=1, device_id=device, device_id_type=MESH)

    @pl.when(other)
    def _():
        greet(me.origin(0)[2])
        greet(me.worker(0)[2])

    for k in range(1, 8):
        greet(me.origin(k)[2])
        greet(me.worker(k)[2])
    expect = 16 - 2 * myself.astype(jnp.int32)
    for ok, device in times + sides:
        @pl.when(ok)
        def _():
            greet(device)
        expect = expect + ok.astype(jnp.int32)

    def pack(which, source):
        for h in range(HEADS):
            block = source[:, :, :, h * HEAD_DIM:(h + 1) * HEAD_DIM].astype(F32)
            block = block.reshape(2, 4, 4, 8, HEAD_DIM)
            block = jnp.transpose(block, (2, 1, 0, 3, 4)).reshape(4, 4, 16, HEAD_DIM)
            packed[which, h] = block.astype(BF16)

    my_rows, my_spot = pl.ds(me.zp * 4, 4), pl.ds(pl.multiple_of(me.core * 16, 16), 16)

    def share(which, first, count, send, recv, k):
        zh, zl, device = me.worker(k)
        if first < 4:
            head, column = 3 * zh + 2 * zl, first
        else:
            head, column = 3 * zh + 1, (2 * zl if which == 2 else zl)
        source = packed.at[which, head, pl.ds(column, count)]
        if which == 2:
            target = qs.at[me.zz, pl.ds(first, count), my_rows, my_spot]
        else:
            target = kv.at[which, 1, 1 + me.zz, pl.ds(first, count), my_rows, my_spot]
        return source, target, pltpu.make_async_remote_copy(
            source, target, send.at[k], recv, device_id=device, device_id_type=MESH)

    def spread(which, first, count, send, recv):
        source, target, remote = share(which, first, count, send, recv, 0)

        @pl.when(myself)
        def _():
            pltpu.make_async_copy(source, target, recv).start()

        @pl.when(other)
        def _():
            remote.start()

        def step(k, _):
            share(which, first, count, send, recv, k)[2].start()
            return 0

        lax.fori_loop(1, 8, step, 0)

    def spread_sent(which, first, count, send, recv):
        pl.when(other)(lambda: share(which, first, count, send, recv, 0)[2].wait_send())

        def step(k, _):
            share(which, first, count, send, recv, k)[2].wait_send()
            return 0

        lax.fori_loop(1, 8, step, 0)

    def chunk_share(c):
        which, first, count = CHUNKS[c]
        return which, first, count, send_kv.at[c], recv_kv.at[c]

    def query_share(i):
        first, count = QUERY_GROUPS[i]
        return 2, first, count, send_q.at[i], recv_q.at[i]

    def y_copy(c, d):
        which, first, count = CHUNKS[c]
        source = kv.at[which, 1, pl.ds(1, 2), pl.ds(first, count)]
        target = kv.at[which, 2 * d, pl.ds(1, 2), pl.ds(first, count)]
        return pltpu.make_async_remote_copy(
            source, target, send_y.at[c, d], recv_y.at[c, d], device_id=times[d][1], device_id_type=MESH)

    def x_copy(c, d, dt):
        which, first, count = CHUNKS[c]
        source = kv.at[which, dt, 2 - d, pl.ds(first, count)]
        target = kv.at[which, dt, 3 * d, pl.ds(first, count)]
        return pltpu.make_async_remote_copy(
            source, target, send_x.at[c, d, dt], recv_x.at[c, d, dt], device_id=sides[d][1], device_id_type=MESH)

    filled = (times[1][0], True, times[0][0])

    def send_x_part(c, dt):
        for d in range(2):
            pl.when(sides[d][0] & filled[dt])(lambda: x_copy(c, d, dt).start())

    def after_own(c):
        which, first, count = CHUNKS[c]
        whole = kv.at[which, 1, pl.ds(1, 2), pl.ds(first, count)]
        pltpu.make_async_copy(whole, whole, recv_kv.at[c]).wait()
        for d in range(2):
            pl.when(times[d][0])(lambda: y_copy(c, d).start())
        send_x_part(c, 1)

    def after_y(c):
        for d in range(2):
            pl.when(filled[2 * d])(lambda: y_copy(c, d).wait_recv())
            send_x_part(c, 2 * d)

    def after_x(c):
        for d in range(2):
            for dt in range(3):
                pl.when(sides[1 - d][0] & filled[dt])(lambda: x_copy(c, d, dt).wait_recv())

    def queries_here(i):
        first, count = QUERY_GROUPS[i]
        whole = qs.at[:, pl.ds(first, count)]
        pltpu.make_async_copy(whole, whole, recv_q.at[i]).wait()

    limits = []
    for row in range(4):
        tile = 2 * me.x - 1 + row
        inside = (tile >= 0) & (tile < 8)
        limits.append(jnp.where(inside, row_valid[jnp.clip(tile, 0, 7)], 0))

    def attend(wave, r, slot, base, count, column, first):
        flat = ((me.t * 8 + 2 * me.x + r) * 4 + column) * 3
        off_t, off_r, off_c = offsets[flat], offsets[flat + 1], offsets[flat + 2]
        query = qs[r, slot].reshape(256, HEAD_DIM)
        if wave == 0:
            near = [(1, 1, limits[1]), (1, 2, limits[2])]
        elif wave == 1:
            near = [(dt, row, limits[row]) for dt in (0, 2) for row in (1, 2)]
        else:
            near = [(dt, 3 * r, jnp.where(r == 0, limits[0], limits[3])) for dt in (0, 1, 2)]
        less = []
        for dt, row, valid in near:
            dr = row - r - 1
            ok = ((dt - 1) * off_t >= 0) & (dr * off_r >= 0)
            if dt != 1:
                ok = ok & filled[dt]
            for j in range(count):
                limit = jnp.where(ok & ((first + j) * off_c >= 0), valid, 0)
                less.append([jnp.where(limit > row_in, 0.0, -jnp.inf).astype(F32) for row_in in range(8)])
        best = jnp.full((8, 256), -jnp.inf, F32)
        for i, (dt, row, _) in enumerate(near):
            keys = kv[0, dt, row, pl.ds(base, count)].reshape(count * 256, HEAD_DIM)
            s = lax.dot_general(keys, query, (((1,), (1,)), ((), ())), preferred_element_type=F32)
            scores[i, pl.ds(0, count * 256)] = s
            highest = jnp.max(s.reshape(count * 8, 4, 8, 256), axis=1)
            for j in range(count):
                for n in range(8):
                    best = jnp.maximum(best, highest[j * 8 + n] + less[i * count + j][n])
        best = jnp.broadcast_to(jnp.max(best, axis=0, keepdims=True), (8, 256))
        if wave == 0:
            summed = jnp.zeros((8, 256), F32)
            held = jnp.zeros((HEAD_DIM, 256), F32)
        else:
            before = top[r, slot]
            best = jnp.maximum(best, before)
            fade = jnp.exp2((before - best) * SCALE)
            summed = total[r, slot] * fade
            held = gathered[r, slot] * fade[0:1]
        shift = best * SCALE
        for i, (dt, row, _) in enumerate(near):
            parts = []
            for j in range(count):
                for n in range(8):
                    s = scores[i, pl.ds(j * 256 + n * 32, 32)].reshape(4, 8, 256)
                    p = jnp.exp2(s * SCALE - (shift - less[i * count + j][n])[None])
                    summed = summed + jnp.sum(p, axis=0)
                    parts.append(p.reshape(32, 256).astype(BF16))
            weights = jnp.concatenate(parts, axis=0)
            value = kv[1, dt, row, pl.ds(base, count)].reshape(count * 256, HEAD_DIM)
            held = held + lax.dot_general(value, weights, (((0,), (0,)), ((), ())), preferred_element_type=F32)
        if wave < 2:
            top[r, slot] = best
            total[r, slot] = summed
            gathered[r, slot] = held
        else:
            result = held / jnp.sum(summed, axis=0, keepdims=True)
            result = result.T.reshape(8, 32, HEAD_DIM)
            keep = lax.broadcasted_iota(jnp.int32, (8, 1, HEAD_DIM), 0) < jnp.where(r == 0, limits[1], limits[2])
            tiles[r, slot] = jnp.where(keep, result, 0.0).astype(BF16)

    def whole_head(wave):
        def step(i, _):
            r, right = div(i, 2), rem(i, 2)
            attend(wave, r, 1 + right, right, 3, 1 + right, -1)
            attend(wave, r, 3 * right, 2 * right, 2, 3 * right, -right)
            return 0

        lax.fori_loop(0, 4, step, 0)

    def shared_head(wave):
        def step(r, _):
            attend(wave, r, 5 - me.zl, 4, 3, 1 + me.zl, -1)
            attend(wave, r, 4 + me.zl, 4 + me.zl, 2, 3 * me.zl, -me.zl)
            return 0

        lax.fori_loop(0, 2, step, 0)

    def result_share(part, k):
        zh, core, device = me.origin(k)
        rows, spot = pl.ds(rem(zh, 2) * 4, 4), pl.ds(pl.multiple_of(core * 16, 16), 16)
        if part == 0:
            source = tiles.at[div(zh, 2), pl.ds(0, 4), rows, spot]
            target = landed.at[3 * me.zh + 2 * me.zl]
        else:
            source = tiles.at[div(zh, 2), pl.ds(4, 2), rows, spot]
            target = landed.at[3 * me.zh + 1, pl.ds(2 * me.zl, 2)]
        return source, target, pltpu.make_async_remote_copy(
            source, target, send_o.at[part, k], recv_o.at[part], device_id=device, device_id_type=MESH)

    def give_back(part):
        source, target, remote = result_share(part, 0)

        @pl.when(myself)
        def _():
            pltpu.make_async_copy(source, target, recv_o.at[part]).start()

        @pl.when(other)
        def _():
            remote.start()

        def step(k, _):
            result_share(part, k)[2].start()
            return 0

        lax.fori_loop(1, 8, step, 0)

    def given_back(part):
        pl.when(other)(lambda: result_share(part, 0)[2].wait_send())

        def step(k, _):
            result_share(part, k)[2].wait_send()
            return 0

        lax.fori_loop(1, 8, step, 0)

    def unpack(part):
        heads = [h for h in range(HEADS) if (h % 3 == 1) == (part == 1)]
        whole = landed.at[pl.ds(0, 8 if part == 0 else 4)]
        pltpu.make_async_copy(whole, whole, recv_o.at[part]).wait()
        for h in heads:
            block = landed[h].astype(F32).reshape(4, 4, 2, 8, HEAD_DIM)
            block = jnp.transpose(block, (2, 1, 0, 3, 4)).reshape(2, 4, 32, HEAD_DIM)
            out[:, :, :, h * HEAD_DIM:(h + 1) * HEAD_DIM] = block.astype(BF16)

    pack(0, k_in)
    pl.semaphore_wait(barrier, expect)
    spread(*chunk_share(0))
    pack(1, v_in)
    spread(*chunk_share(1))
    spread(*chunk_share(2))
    spread(*chunk_share(3))
    pack(2, q_in)
    spread(*query_share(0))
    spread(*chunk_share(4))
    spread(*chunk_share(5))
    spread(*query_share(1))
    for c in range(4):
        after_own(c)
        if c:
            after_y(c - 1)
    after_y(3)
    queries_here(0)
    whole_head(0)
    after_own(4)
    whole_head(1)
    after_y(4)
    after_own(5)
    for c in range(4):
        after_x(c)
    after_y(5)
    whole_head(2)
    give_back(0)
    queries_here(1)
    shared_head(0)
    shared_head(1)
    after_x(4)
    after_x(5)
    shared_head(2)
    give_back(1)
    unpack(0)
    unpack(1)
    for c in range(6):
        spread_sent(*chunk_share(c))
        for d in range(2):
            pl.when(times[d][0])(lambda: y_copy(c, d).wait_send())
            for dt in range(3):
                pl.when(sides[d][0] & filled[dt])(lambda: x_copy(c, d, dt).wait_send())
    for i in range(2):
        spread_sent(*query_share(i))
        given_back(i)


def shards(queries, keys, values, win_off, row_valid):
    dma = pltpu.SemaphoreType.DMA
    smem = pl.BlockSpec(memory_space=pltpu.SMEM)
    vmem = pl.BlockSpec(memory_space=pltpu.VMEM)
    return pl.pallas_call(
        kernel,
        out_shape=jax.ShapeDtypeStruct(queries.shape, BF16),
        in_specs=[smem, smem, vmem, vmem, vmem],
        out_specs=vmem,
        scratch_shapes=[
            pltpu.VMEM((2, 3, 4, 7, 8, 32, HEAD_DIM), BF16),
            pltpu.VMEM((2, 6, 8, 32, HEAD_DIM), BF16),
            pltpu.VMEM((3, HEADS, 4, 4, 16, HEAD_DIM), BF16),
            pltpu.VMEM((2, 6, 8, 32, HEAD_DIM), BF16),
            pltpu.VMEM((HEADS, 4, 4, 16, HEAD_DIM), BF16),
            pltpu.VMEM((4, 768, 256), F32),
            pltpu.VMEM((2, 6, 8, 256), F32),
            pltpu.VMEM((2, 6, 8, 256), F32),
            pltpu.VMEM((2, 6, HEAD_DIM, 256), F32),
            dma((6, 8)), dma((2, 8)), dma((6, 2)), dma((6, 2, 3)), dma((2, 8)),
            dma((6,)), dma((2,)), dma((6, 2)), dma((6, 2, 3)), dma((2,)),
        ],
        compiler_params=pltpu.CompilerParams(
            collective_id=0, has_side_effects=True, vmem_limit_bytes=VMEM_LIMIT),
    )(win_off.reshape(-1), row_valid, queries, keys, values)


def solution(mesh):
    return jax.shard_map(
        shards,
        mesh=mesh,
        in_specs=(
            P("tm", "rows", None, None),
            P("tm", "rows", None, None),
            P("tm", "rows", None, None),
            P(),
            P(),
        ),
        out_specs=P("tm", "rows", None, None),
        check_vma=False,
    )
```

time: 802 us -> 109 us (0.14)
  the two profiles are of different devices: /device:TPU:19 before, /device:TPU:13 now
where the time goes in v2:
time: 109 us
  Pallas kernels  105 us (96%)
  local copies, waits for them, and re-layouts  3.93 us (4%)
    pallas_call x1, Pallas kernels, shards(): pl.pallas_call(kernel, out_shape=jax.ShapeDtypeStruct(queries.shape, BF16...  105 us
    unnamed x2, local copies, waits for them, and re-layouts  3.12 us

profile of v2, /device:TPU:13, one launch (start us, length us, event | category | flops | bytes accessed | tf_op | source)
XLA Modules:
  0.0 109.2 jit_solution(9398213193673248883)
XLA Ops:
  0.0 1.1 copy.6
  1.1 0.8 reshape.3.offsets
  1.9 105.3 %shard_map.55 = bf16[2,4,32,1536]{3,2,1,0:T(8,128)(2,1)} custom-call(s32[768]{0:T(1024)} %reshape.3.offsets, s32[8]{0:T(128)} %row_valid.1, bf16[2,4,32,1536]{3,2,1,0:T(8,128)(2,1)} %q_in.1, bf16[2,4,32,1536]{3,2,1,0:T(8,128)(2,1)} %k_in.1, bf16[2,4,32,1536]{3,2,1,0:T(8,128)(2,1)} %v_in.1), custom_call_target="tpu_custom_call" | custom-call | tf_op jit(solution)/shard_map/pallas_call | solution.py:389
  107.1 2.1 %copy.8 = bf16[2,4,32,1536]{3,2,1,0:T(8,128)(2,1)} copy(bf16[2,4,32,1536]{3,2,1,0:T(8,128)(2,1)} %shard_map.55) | data formatting | bytes 1572864

commit v3 on v2

--- a/solution.py
+++ b/solution.py
@@ -65,10 +65,11 @@
 GROUPS = ((0, 2), (2, 2), (4, 3))
 CHUNKS = tuple((which, first, count) for first, count in GROUPS for which in (0, 1))
 QUERY_GROUPS = ((0, 4), (4, 2))
-
-
-def kernel(offsets, row_valid, q_in, k_in, v_in, out, kv, qs, packed, tiles, landed, scores, top, total, gathered,
-           send_kv, send_q, send_y, send_x, send_o, recv_kv, recv_q, recv_y, recv_x, recv_o):
+ROWS_FIRST = 5
+
+
+def kernel(offsets, row_valid, q_in, k_in, v_in, landed, kv, qs, packed, tiles, scores, top, total, gathered,
+           send_kv, send_q, send_y, send_x, send_c, send_o, recv_kv, recv_q, recv_y, recv_x, recv_c, recv_o):
     me = Place()
     times = [me.time_neighbour(s) for s in (1, -1)]
     sides = [me.row_neighbour(s) for s in (1, -1)]
@@ -199,6 +200,29 @@
             for dt in range(3):
                 pl.when(sides[1 - d][0] & filled[dt])(lambda: x_copy(c, d, dt).wait_recv())
 
+    def corner_copy(d, side):
+        which, first, count = CHUNKS[ROWS_FIRST]
+        source = kv.at[which, 1, 3 * side, pl.ds(first, count)]
+        target = kv.at[which, 2 * d, 3 * side, pl.ds(first, count)]
+        return pltpu.make_async_remote_copy(
+            source, target, send_c.at[d, side], recv_c.at[d, side], device_id=times[d][1], device_id_type=MESH)
+
+    def send_corners():
+        for side in range(2):
+            here = sides[1 - side][0]
+            pl.when(here)(lambda: x_copy(ROWS_FIRST, side, 1).wait_recv())
+            for d in range(2):
+                pl.when(here & times[d][0])(lambda: corner_copy(d, side).start())
+
+    def own_y_here():
+        for d in range(2):
+            pl.when(filled[2 * d])(lambda: y_copy(ROWS_FIRST, d).wait_recv())
+
+    def corners_here():
+        for side in range(2):
+            for d in range(2):
+                pl.when(sides[1 - side][0] & filled[2 * d])(lambda: corner_copy(d, side).wait_recv())
+
     def queries_here(i):
         first, count = QUERY_GROUPS[i]
         whole = qs.at[:, pl.ds(first, count)]
@@ -211,8 +235,7 @@
         limits.append(jnp.where(inside, row_valid[jnp.clip(tile, 0, 7)], 0))
 
     def attend(wave, r, slot, base, count, column, first):
-        flat = ((me.t * 8 + 2 * me.x + r) * 4 + column) * 3
-        off_t, off_r, off_c = offsets[flat], offsets[flat + 1], offsets[flat + 2]
+        off_t, off_r, off_c = [offsets[me.t, i, column, 2 * me.x + r] for i in range(3)]
         query = qs[r, slot].reshape(256, HEAD_DIM)
         if wave == 0:
             near = [(1, 1, limits[1]), (1, 2, limits[2])]
@@ -270,69 +293,78 @@
             keep = lax.broadcasted_iota(jnp.int32, (8, 1, HEAD_DIM), 0) < jnp.where(r == 0, limits[1], limits[2])
             tiles[r, slot] = jnp.where(keep, result, 0.0).astype(BF16)
 
-    def whole_head(wave):
-        def step(i, _):
-            r, right = div(i, 2), rem(i, 2)
-            attend(wave, r, 1 + right, right, 3, 1 + right, -1)
-            attend(wave, r, 3 * right, 2 * right, 2, 3 * right, -right)
-            return 0
-
-        lax.fori_loop(0, 4, step, 0)
-
-    def shared_head(wave):
+    def whole_head(wave, then=None):
+        def step(r, _):
+            def half(right, _):
+                attend(wave, r, 1 + right, right, 3, 1 + right, -1)
+                attend(wave, r, 3 * right, 2 * right, 2, 3 * right, -right)
+                return 0
+
+            lax.fori_loop(0, 2, half, 0)
+            if then is not None:
+                then(r)
+            return 0
+
+        lax.fori_loop(0, 2, step, 0)
+
+    def shared_head(wave, then=None):
         def step(r, _):
             attend(wave, r, 5 - me.zl, 4, 3, 1 + me.zl, -1)
             attend(wave, r, 4 + me.zl, 4 + me.zl, 2, 3 * me.zl, -me.zl)
+            if then is not None:
+                then(r)
             return 0
 
         lax.fori_loop(0, 2, step, 0)
 
-    def result_share(part, k):
-        zh, core, device = me.origin(k)
-        rows, spot = pl.ds(rem(zh, 2) * 4, 4), pl.ds(pl.multiple_of(core * 16, 16), 16)
+    def result_share(part, r, j):
+        zp, core = rem(me.zp + div(j, 2), 2), rem(me.core + rem(j, 2), 2)
+        device = (me.core * 8 + me.y * 2 + core, me.x * 4 + r * 2 + zp)
+        rows, spot = pl.ds(zp * 4, 4), pl.ds(pl.multiple_of(core * 16, 16), 16)
         if part == 0:
-            source = tiles.at[div(zh, 2), pl.ds(0, 4), rows, spot]
+            source = tiles.at[r, pl.ds(0, 4), rows, spot]
             target = landed.at[3 * me.zh + 2 * me.zl]
         else:
-            source = tiles.at[div(zh, 2), pl.ds(4, 2), rows, spot]
+            source = tiles.at[r, pl.ds(4, 2), rows, spot]
             target = landed.at[3 * me.zh + 1, pl.ds(2 * me.zl, 2)]
         return source, target, pltpu.make_async_remote_copy(
-            source, target, send_o.at[part, k], recv_o.at[part], device_id=device, device_id_type=MESH)
-
-    def give_back(part):
-        source, target, remote = result_share(part, 0)
-
-        @pl.when(myself)
+            source, target, send_o.at[part, r, j], recv_o.at[part], device_id=device, device_id_type=MESH)
+
+    def give_back(part, r):
+        mine = myself & (r == me.zz)
+        source, target, remote = result_share(part, r, jnp.int32(0))
+
+        @pl.when(mine)
         def _():
             pltpu.make_async_copy(source, target, recv_o.at[part]).start()
 
-        @pl.when(other)
+        @pl.when(jnp.logical_not(mine))
         def _():
             remote.start()
 
-        def step(k, _):
-            result_share(part, k)[2].start()
-            return 0
-
-        lax.fori_loop(1, 8, step, 0)
+        def step(j, _):
+            result_share(part, r, j)[2].start()
+            return 0
+
+        lax.fori_loop(1, 4, step, 0)
 
     def given_back(part):
-        pl.when(other)(lambda: result_share(part, 0)[2].wait_send())
-
-        def step(k, _):
-            result_share(part, k)[2].wait_send()
-            return 0
-
-        lax.fori_loop(1, 8, step, 0)
-
-    def unpack(part):
-        heads = [h for h in range(HEADS) if (h % 3 == 1) == (part == 1)]
+        def each(r, _):
+            mine = myself & (r == me.zz)
+            pl.when(jnp.logical_not(mine))(lambda: result_share(part, r, jnp.int32(0))[2].wait_send())
+
+            def step(j, _):
+                result_share(part, r, j)[2].wait_send()
+                return 0
+
+            lax.fori_loop(1, 4, step, 0)
+            return 0
+
+        lax.fori_loop(0, 2, each, 0)
+
+    def landed_here(part):
         whole = landed.at[pl.ds(0, 8 if part == 0 else 4)]
         pltpu.make_async_copy(whole, whole, recv_o.at[part]).wait()
-        for h in heads:
-            block = landed[h].astype(F32).reshape(4, 4, 2, 8, HEAD_DIM)
-            block = jnp.transpose(block, (2, 1, 0, 3, 4)).reshape(2, 4, 32, HEAD_DIM)
-            out[:, :, :, h * HEAD_DIM:(h + 1) * HEAD_DIM] = block.astype(BF16)
 
     pack(0, k_in)
     pl.semaphore_wait(barrier, expect)
@@ -353,60 +385,72 @@
     after_y(3)
     queries_here(0)
     whole_head(0)
-    after_own(4)
-    whole_head(1)
+    whole_head(1, lambda r: pl.when(r == 0)(lambda: after_own(4)))
     after_y(4)
     after_own(5)
     for c in range(4):
         after_x(c)
-    after_y(5)
-    whole_head(2)
-    give_back(0)
+    whole_head(2, lambda r: give_back(0, r))
+    send_corners()
     queries_here(1)
     shared_head(0)
+    own_y_here()
     shared_head(1)
     after_x(4)
-    after_x(5)
-    shared_head(2)
-    give_back(1)
-    unpack(0)
-    unpack(1)
+    corners_here()
+    shared_head(2, lambda r: give_back(1, r))
+    landed_here(0)
+    landed_here(1)
     for c in range(6):
         spread_sent(*chunk_share(c))
         for d in range(2):
             pl.when(times[d][0])(lambda: y_copy(c, d).wait_send())
-            for dt in range(3):
+            for dt in ((1,) if c == ROWS_FIRST else range(3)):
                 pl.when(sides[d][0] & filled[dt])(lambda: x_copy(c, d, dt).wait_send())
     for i in range(2):
         spread_sent(*query_share(i))
         given_back(i)
+        for d in range(2):
+            pl.when(sides[1 - i][0] & times[d][0])(lambda: corner_copy(d, i).wait_send())
+
+
+def unpack_kernel(landed, out):
+    for h in range(HEADS):
+        block = landed[h].astype(F32).reshape(4, 4, 2, 8, HEAD_DIM)
+        block = jnp.transpose(block, (2, 1, 0, 3, 4)).reshape(2, 4, 32, HEAD_DIM)
+        out[:, :, :, h * HEAD_DIM:(h + 1) * HEAD_DIM] = block.astype(BF16)
 
 
 def shards(queries, keys, values, win_off, row_valid):
     dma = pltpu.SemaphoreType.DMA
     smem = pl.BlockSpec(memory_space=pltpu.SMEM)
     vmem = pl.BlockSpec(memory_space=pltpu.VMEM)
-    return pl.pallas_call(
+    landed = pl.pallas_call(
         kernel,
-        out_shape=jax.ShapeDtypeStruct(queries.shape, BF16),
+        out_shape=jax.ShapeDtypeStruct((HEADS, 4, 4, 16, HEAD_DIM), BF16),
         in_specs=[smem, smem, vmem, vmem, vmem],
-        out_specs=vmem,
+        out_specs=pl.BlockSpec(memory_space=pl.ANY),
         scratch_shapes=[
             pltpu.VMEM((2, 3, 4, 7, 8, 32, HEAD_DIM), BF16),
             pltpu.VMEM((2, 6, 8, 32, HEAD_DIM), BF16),
             pltpu.VMEM((3, HEADS, 4, 4, 16, HEAD_DIM), BF16),
             pltpu.VMEM((2, 6, 8, 32, HEAD_DIM), BF16),
-            pltpu.VMEM((HEADS, 4, 4, 16, HEAD_DIM), BF16),
             pltpu.VMEM((4, 768, 256), F32),
             pltpu.VMEM((2, 6, 8, 256), F32),
             pltpu.VMEM((2, 6, 8, 256), F32),
             pltpu.VMEM((2, 6, HEAD_DIM, 256), F32),
-            dma((6, 8)), dma((2, 8)), dma((6, 2)), dma((6, 2, 3)), dma((2, 8)),
-            dma((6,)), dma((2,)), dma((6, 2)), dma((6, 2, 3)), dma((2,)),
+            dma((6, 8)), dma((2, 8)), dma((6, 2)), dma((6, 2, 3)), dma((2, 2)), dma((2, 2, 4)),
+            dma((6,)), dma((2,)), dma((6, 2)), dma((6, 2, 3)), dma((2, 2)), dma((2,)),
         ],
         compiler_params=pltpu.CompilerParams(
             collective_id=0, has_side_effects=True, vmem_limit_bytes=VMEM_LIMIT),
-    )(win_off.reshape(-1), row_valid, queries, keys, values)
+    )(jnp.transpose(win_off, (0, 3, 2, 1)), row_valid, queries, keys, values)
+    return pl.pallas_call(
+        unpack_kernel,
+        out_shape=jax.ShapeDtypeStruct(queries.shape, BF16),
+        in_specs=[vmem],
+        out_specs=vmem,
+    )(landed)
 
 
 def solution(mesh):

time: 109 us -> 101 us (0.927)
  the two profiles are of different devices: /device:TPU:13 before, /device:TPU:19 now
where the time goes in v3:
time: 101 us; the launch traced here: 99.7 us
  Pallas kernels  99.7 us (99%)
    pallas_call x1, Pallas kernels, shards(): pl.pallas_call(kernel, out_shape=jax.ShapeDtypeStruct((HEADS, 4, 4, 16, H...  97.5 us
    pallas_call x1, Pallas kernels, shards(): pl.pallas_call(unpack_kernel, out_shape=jax.ShapeDtypeStruct(queries.shap...  2.15 us

profile of v3, /device:TPU:19, one launch (start us, length us, event | category | flops | bytes accessed | tf_op | source)
XLA Modules:
  0.0 99.7 jit_solution(1566471189110244035)
XLA Ops:
  0.0 97.5 %shard_map.55.landed = bf16[12,4,4,16,128]{4,3,2,1,0:T(8,128)(2,1)} custom-call(s32[8,3,4,8]{3,2,1,0:T(4,128)} %bitcast.1, s32[8]{0:T(128)} %row_valid.1, bf16[2,4,32,1536]{3,2,1,0:T(8,128)(2,1)} %q_in.1, bf16[2,4,32,1536]{3,2,1,0:T(8,128)(2,1)} %k_in.1, bf16[2,4,32,1536]{3,2,1,0:T(8,128)(2,1)} %v_in.1), custom_call_target="tpu_custom_call" | custom-call | tf_op jit(solution)/shard_map/pallas_call | solution.py:428
  97.5 2.1 %shard_map.56 = bf16[2,4,32,1536]{3,2,1,0:T(8,128)(2,1)} custom-call(bf16[12,4,4,16,128]{4,3,2,1,0:T(8,128)(2,1)} %shard_map.55.landed), custom_call_target="tpu_custom_call" | custom-call | tf_op jit(solution)/shard_map/pallas_call | solution.py:448

commit v4 on v3

--- a/solution.py
+++ b/solution.py
@@ -62,10 +62,12 @@
         return ok, (self.zl * 8 + self.y * 2 + self.core, x * 4 + self.zh)
 
 
-GROUPS = ((0, 2), (2, 2), (4, 3))
-CHUNKS = tuple((which, first, count) for first, count in GROUPS for which in (0, 1))
+GROUPS = ((0, 2), (2, 2), (6, 1), (4, 2))
+CHUNKS = tuple((which, first, count) for which, (first, count) in (
+    (0, GROUPS[0]), (1, GROUPS[0]), (0, GROUPS[1]), (1, GROUPS[1]),
+    (0, GROUPS[2]), (0, GROUPS[3]), (1, GROUPS[2]), (1, GROUPS[3])))
 QUERY_GROUPS = ((0, 4), (4, 2))
-ROWS_FIRST = 5
+ROWS_FIRST = (4, 6)
 
 
 def kernel(offsets, row_valid, q_in, k_in, v_in, landed, kv, qs, packed, tiles, scores, top, total, gathered,
@@ -119,7 +121,7 @@
         if first < 4:
             head, column = 3 * zh + 2 * zl, first
         else:
-            head, column = 3 * zh + 1, (2 * zl if which == 2 else zl)
+            head, column = 3 * zh + 1, (2 * zl if which == 2 else zl) + first - 4
         source = packed.at[which, head, pl.ds(column, count)]
         if which == 2:
             target = qs.at[me.zz, pl.ds(first, count), my_rows, my_spot]
@@ -200,28 +202,29 @@
             for dt in range(3):
                 pl.when(sides[1 - d][0] & filled[dt])(lambda: x_copy(c, d, dt).wait_recv())
 
-    def corner_copy(d, side):
-        which, first, count = CHUNKS[ROWS_FIRST]
+    def corner_copy(c, d, side):
+        which, first, count = CHUNKS[c]
         source = kv.at[which, 1, 3 * side, pl.ds(first, count)]
         target = kv.at[which, 2 * d, 3 * side, pl.ds(first, count)]
+        i = ROWS_FIRST.index(c)
         return pltpu.make_async_remote_copy(
-            source, target, send_c.at[d, side], recv_c.at[d, side], device_id=times[d][1], device_id_type=MESH)
-
-    def send_corners():
+            source, target, send_c.at[i, d, side], recv_c.at[i, d, side], device_id=times[d][1], device_id_type=MESH)
+
+    def send_corners(c):
         for side in range(2):
             here = sides[1 - side][0]
-            pl.when(here)(lambda: x_copy(ROWS_FIRST, side, 1).wait_recv())
+            pl.when(here)(lambda: x_copy(c, side, 1).wait_recv())
             for d in range(2):
-                pl.when(here & times[d][0])(lambda: corner_copy(d, side).start())
-
-    def own_y_here():
+                pl.when(here & times[d][0])(lambda: corner_copy(c, d, side).start())
+
+    def own_y_here(c):
         for d in range(2):
-            pl.when(filled[2 * d])(lambda: y_copy(ROWS_FIRST, d).wait_recv())
-
-    def corners_here():
+            pl.when(filled[2 * d])(lambda: y_copy(c, d).wait_recv())
+
+    def corners_here(c):
         for side in range(2):
             for d in range(2):
-                pl.when(sides[1 - side][0] & filled[2 * d])(lambda: corner_copy(d, side).wait_recv())
+                pl.when(sides[1 - side][0] & filled[2 * d])(lambda: corner_copy(c, d, side).wait_recv())
 
     def queries_here(i):
         first, count = QUERY_GROUPS[i]
@@ -254,13 +257,16 @@
                 less.append([jnp.where(limit > row_in, 0.0, -jnp.inf).astype(F32) for row_in in range(8)])
         best = jnp.full((8, 256), -jnp.inf, F32)
         for i, (dt, row, _) in enumerate(near):
-            keys = kv[0, dt, row, pl.ds(base, count)].reshape(count * 256, HEAD_DIM)
-            s = lax.dot_general(keys, query, (((1,), (1,)), ((), ())), preferred_element_type=F32)
-            scores[i, pl.ds(0, count * 256)] = s
-            highest = jnp.max(s.reshape(count * 8, 4, 8, 256), axis=1)
             for j in range(count):
+                keys = kv[0, dt, row, base + j].reshape(256, HEAD_DIM)
+                s = lax.dot_general(keys, query, (((1,), (1,)), ((), ())), preferred_element_type=F32)
+                scores[3 - count, i, pl.ds(j * 256, 256)] = s
+                highest = jnp.max(s.reshape(8, 4, 8, 256), axis=1)
                 for n in range(8):
-                    best = jnp.maximum(best, highest[j * 8 + n] + less[i * count + j][n])
+                    best = jnp.maximum(best, highest[n] + less[i * count + j][n])
+        return lambda: weigh(wave, r, slot, base, count, near, less, best)
+
+    def weigh(wave, r, slot, base, count, near, less, best):
         best = jnp.broadcast_to(jnp.max(best, axis=0, keepdims=True), (8, 256))
         if wave == 0:
             summed = jnp.zeros((8, 256), F32)
@@ -273,16 +279,16 @@
             held = gathered[r, slot] * fade[0:1]
         shift = best * SCALE
         for i, (dt, row, _) in enumerate(near):
-            parts = []
             for j in range(count):
+                parts = []
                 for n in range(8):
-                    s = scores[i, pl.ds(j * 256 + n * 32, 32)].reshape(4, 8, 256)
+                    s = scores[3 - count, i, pl.ds(j * 256 + n * 32, 32)].reshape(4, 8, 256)
                     p = jnp.exp2(s * SCALE - (shift - less[i * count + j][n])[None])
                     summed = summed + jnp.sum(p, axis=0)
                     parts.append(p.reshape(32, 256).astype(BF16))
-            weights = jnp.concatenate(parts, axis=0)
-            value = kv[1, dt, row, pl.ds(base, count)].reshape(count * 256, HEAD_DIM)
-            held = held + lax.dot_general(value, weights, (((0,), (0,)), ((), ())), preferred_element_type=F32)
+                weights = jnp.concatenate(parts, axis=0)
+                value = kv[1, dt, row, base + j].reshape(256, HEAD_DIM)
+                held = held + lax.dot_general(value, weights, (((0,), (0,)), ((), ())), preferred_element_type=F32)
         if wave < 2:
             top[r, slot] = best
             total[r, slot] = summed
@@ -296,8 +302,10 @@
     def whole_head(wave, then=None):
         def step(r, _):
             def half(right, _):
-                attend(wave, r, 1 + right, right, 3, 1 + right, -1)
-                attend(wave, r, 3 * right, 2 * right, 2, 3 * right, -right)
+                wide = attend(wave, r, 1 + right, right, 3, 1 + right, -1)
+                edge = attend(wave, r, 3 * right, 2 * right, 2, 3 * right, -right)
+                wide()
+                edge()
                 return 0
 
             lax.fori_loop(0, 2, half, 0)
@@ -309,8 +317,10 @@
 
     def shared_head(wave, then=None):
         def step(r, _):
-            attend(wave, r, 5 - me.zl, 4, 3, 1 + me.zl, -1)
-            attend(wave, r, 4 + me.zl, 4 + me.zl, 2, 3 * me.zl, -me.zl)
+            wide = attend(wave, r, 5 - me.zl, 4, 3, 1 + me.zl, -1)
+            edge = attend(wave, r, 4 + me.zl, 4 + me.zl, 2, 3 * me.zl, -me.zl)
+            wide()
+            edge()
             if then is not None:
                 then(r)
             return 0
@@ -375,8 +385,8 @@
     spread(*chunk_share(3))
     pack(2, q_in)
     spread(*query_share(0))
-    spread(*chunk_share(4))
-    spread(*chunk_share(5))
+    for c in range(4, 8):
+        spread(*chunk_share(c))
     spread(*query_share(1))
     for c in range(4):
         after_own(c)
@@ -385,33 +395,55 @@
     after_y(3)
     queries_here(0)
     whole_head(0)
-    whole_head(1, lambda r: pl.when(r == 0)(lambda: after_own(4)))
-    after_y(4)
-    after_own(5)
+
+    def keys_on(r):
+        @pl.when(r == 0)
+        def _():
+            after_own(4)
+            after_own(5)
+
+    whole_head(1, keys_on)
+    send_corners(4)
+    after_own(6)
     for c in range(4):
         after_x(c)
-    whole_head(2, lambda r: give_back(0, r))
-    send_corners()
+
+    def values_on(r):
+        give_back(0, r)
+
+        @pl.when(r == 0)
+        def _():
+            after_y(5)
+            after_own(7)
+
+    whole_head(2, values_on)
+    send_corners(6)
     queries_here(1)
     shared_head(0)
-    own_y_here()
+    after_y(7)
+    own_y_here(4)
+    own_y_here(6)
     shared_head(1)
-    after_x(4)
-    corners_here()
+    after_x(5)
+    after_x(7)
+    corners_here(4)
+    corners_here(6)
     shared_head(2, lambda r: give_back(1, r))
     landed_here(0)
     landed_here(1)
-    for c in range(6):
+    for c in range(8):
         spread_sent(*chunk_share(c))
         for d in range(2):
             pl.when(times[d][0])(lambda: y_copy(c, d).wait_send())
-            for dt in ((1,) if c == ROWS_FIRST else range(3)):
+            for dt in ((1,) if c in ROWS_FIRST else range(3)):
                 pl.when(sides[d][0] & filled[dt])(lambda: x_copy(c, d, dt).wait_send())
+            if c in ROWS_FIRST:
+                for side in range(2):
+                    pl.when(sides[1 - side][0] & times[d][0])(lambda: corner_copy(c, d, side).wait_send())
     for i in range(2):
         spread_sent(*query_share(i))
+    for i in range(2):
         given_back(i)
-        for d in range(2):
-            pl.when(sides[1 - i][0] & times[d][0])(lambda: corner_copy(d, i).wait_send())
 
 
 def unpack_kernel(landed, out):
@@ -435,12 +467,12 @@
             pltpu.VMEM((2, 6, 8, 32, HEAD_DIM), BF16),
             pltpu.VMEM((3, HEADS, 4, 4, 16, HEAD_DIM), BF16),
             pltpu.VMEM((2, 6, 8, 32, HEAD_DIM), BF16),
-            pltpu.VMEM((4, 768, 256), F32),
+            pltpu.VMEM((2, 4, 768, 256), F32),
             pltpu.VMEM((2, 6, 8, 256), F32),
             pltpu.VMEM((2, 6, 8, 256), F32),
             pltpu.VMEM((2, 6, HEAD_DIM, 256), F32),
-            dma((6, 8)), dma((2, 8)), dma((6, 2)), dma((6, 2, 3)), dma((2, 2)), dma((2, 2, 4)),
-            dma((6,)), dma((2,)), dma((6, 2)), dma((6, 2, 3)), dma((2, 2)), dma((2,)),
+            dma((8, 8)), dma((2, 8)), dma((8, 2)), dma((8, 2, 3)), dma((2, 2, 2)), dma((2, 2, 4)),
+            dma((8,)), dma((2,)), dma((8, 2)), dma((8, 2, 3)), dma((2, 2, 2)), dma((2,)),
         ],
         compiler_params=pltpu.CompilerParams(
             collective_id=0, has_side_effects=True, vmem_limit_bytes=VMEM_LIMIT),

time: 101 us -> 95.3 us (0.944)
  Pallas kernels: 99.7 us -> 93.7 us
    pallas_call x1, Pallas kernels: 97.5 us -> 91.6 us  [shards(): pl.pallas_call(kernel, out_shape=jax.ShapeDtypeStruct((HEADS, 4, 4, 16, H...]
where the time goes in v4:
time: 95.3 us; the launch traced here: 93.7 us
  Pallas kernels  93.7 us (98%)
    pallas_call x1, Pallas kernels, shards(): pl.pallas_call(kernel, out_shape=jax.ShapeDtypeStruct((HEADS, 4, 4, 16, H...  91.6 us
    pallas_call x1, Pallas kernels, shards(): pl.pallas_call(unpack_kernel, out_shape=jax.ShapeDtypeStruct(queries.shap...  2.15 us

profile of v4, /device:TPU:19, one launch (start us, length us, event | category | flops | bytes accessed | tf_op | source)
XLA Modules:
  0.0 93.7 jit_solution(5803778750265057393)
XLA Ops:
  0.0 91.6 %shard_map.55.landed = bf16[12,4,4,16,128]{4,3,2,1,0:T(8,128)(2,1)} custom-call(s32[8,3,4,8]{3,2,1,0:T(4,128)} %bitcast.1, s32[8]{0:T(128)} %row_valid.1, bf16[2,4,32,1536]{3,2,1,0:T(8,128)(2,1)} %q_in.1, bf16[2,4,32,1536]{3,2,1,0:T(8,128)(2,1)} %k_in.1, bf16[2,4,32,1536]{3,2,1,0:T(8,128)(2,1)} %v_in.1), custom_call_target="tpu_custom_call" | custom-call | tf_op jit(solution)/shard_map/pallas_call | solution.py:460
  91.6 2.1 %shard_map.56 = bf16[2,4,32,1536]{3,2,1,0:T(8,128)(2,1)} custom-call(bf16[12,4,4,16,128]{4,3,2,1,0:T(8,128)(2,1)} %shard_map.55.landed), custom_call_target="tpu_custom_call" | custom-call | tf_op jit(solution)/shard_map/pallas_call | solution.py:480

commit v5 on v4

--- a/solution.py
+++ b/solution.py
@@ -197,10 +197,13 @@
             pl.when(filled[2 * d])(lambda: y_copy(c, d).wait_recv())
             send_x_part(c, 2 * d)
 
+    def side_here(c, side):
+        for dt in range(3):
+            pl.when(sides[1 - side][0] & filled[dt])(lambda: x_copy(c, side, dt).wait_recv())
+
     def after_x(c):
-        for d in range(2):
-            for dt in range(3):
-                pl.when(sides[1 - d][0] & filled[dt])(lambda: x_copy(c, d, dt).wait_recv())
+        for side in range(2):
+            side_here(c, side)
 
     def corner_copy(c, d, side):
         which, first, count = CHUNKS[c]
@@ -221,10 +224,15 @@
         for d in range(2):
             pl.when(filled[2 * d])(lambda: y_copy(c, d).wait_recv())
 
-    def corners_here(c):
-        for side in range(2):
-            for d in range(2):
-                pl.when(sides[1 - side][0] & filled[2 * d])(lambda: corner_copy(c, d, side).wait_recv())
+    def corners_here(c, side):
+        for d in range(2):
+            pl.when(sides[1 - side][0] & filled[2 * d])(lambda: corner_copy(c, d, side).wait_recv())
+
+    def shared_halo_here(side):
+        side_here(5, side)
+        corners_here(4, side)
+        side_here(7, side)
+        corners_here(6, side)
 
     def queries_here(i):
         first, count = QUERY_GROUPS[i]
@@ -317,6 +325,9 @@
 
     def shared_head(wave, then=None):
         def step(r, _):
+            if wave == 2:
+                for side in range(2):
+                    pl.when(r == side)(lambda: shared_halo_here(side))
             wide = attend(wave, r, 5 - me.zl, 4, 3, 1 + me.zl, -1)
             edge = attend(wave, r, 4 + me.zl, 4 + me.zl, 2, 3 * me.zl, -me.zl)
             wide()
@@ -424,10 +435,6 @@
     own_y_here(4)
     own_y_here(6)
     shared_head(1)
-    after_x(5)
-    after_x(7)
-    corners_here(4)
-    corners_here(6)
     shared_head(2, lambda r: give_back(1, r))
     landed_here(0)
     landed_here(1)

time: 95.3 us -> 94 us (0.986)
  no operation moved by 1% of the time
where the time goes in v5:
time: 94 us; the launch traced here: 92.9 us
  Pallas kernels  92.8 us (99%)
    pallas_call x1, Pallas kernels, shards(): pl.pallas_call(kernel, out_shape=jax.ShapeDtypeStruct((HEADS, 4, 4, 16, H...  90.7 us
    pallas_call x1, Pallas kernels, shards(): pl.pallas_call(unpack_kernel, out_shape=jax.ShapeDtypeStruct(queries.shap...  2.15 us

profile of v5, /device:TPU:19, one launch (start us, length us, event | category | flops | bytes accessed | tf_op | source)
XLA Modules:
  0.0 92.9 jit_solution(6226098253014657799)
XLA Ops:
  0.0 90.7 %shard_map.55.landed = bf16[12,4,4,16,128]{4,3,2,1,0:T(8,128)(2,1)} custom-call(s32[8,3,4,8]{3,2,1,0:T(4,128)} %bitcast.1, s32[8]{0:T(128)} %row_valid.1, bf16[2,4,32,1536]{3,2,1,0:T(8,128)(2,1)} %q_in.1, bf16[2,4,32,1536]{3,2,1,0:T(8,128)(2,1)} %k_in.1, bf16[2,4,32,1536]{3,2,1,0:T(8,128)(2,1)} %v_in.1), custom_call_target="tpu_custom_call" | custom-call | tf_op jit(solution)/shard_map/pallas_call | solution.py:467
  90.7 2.1 %shard_map.56 = bf16[2,4,32,1536]{3,2,1,0:T(8,128)(2,1)} custom-call(bf16[12,4,4,16,128]{4,3,2,1,0:T(8,128)(2,1)} %shard_map.55.landed), custom_call_target="tpu_custom_call" | custom-call | tf_op jit(solution)/shard_map/pallas_call | solution.py:487
